TPU v7x, 32 devices: a whole 2x2x4 slice. The times are simulated.
32 devices in a mesh: gx: 8 (over z, y), gy: 4 (over x, core).
Axes of the slice: x: 2, y: 2, z: 4, core: 2. Of those that a mesh axis runs over, the one named last changes fastest.
Arguments:
- actuator_mask: int32 [8, 32, 32, 128], P(None, 'gx', 'gy'), may hold values 0 or 1
- forcing: float32 [8, 4, 32, 32, 128], P(None, None, 'gx', 'gy'), may hold values from -18 to 18
- base_flow: float32 [3, 32, 32, 128], P(None, 'gx', 'gy'), may hold values from -0.3 to 0.3
- base_shear: float32 [3, 3, 32, 32, 128], P(None, None, 'gx', 'gy'), may hold values from -1.5 to 1.5
Outputs:
- q_basis: float32 [72, 4, 32, 32, 128], P(None, None, 'gx', 'gy')
- r_factor: float32 [72, 72], replicated
- column_rms: float32 [72], replicated
All inputs are finite; a program needn't handle non-finite values. No bound on the sum of `actuator_mask` on one device may be relied on, other than what follows from the above.
Results may differ from a plain program's by a relative error of at most 0.004.
Values sent between devices are 32-bit elements; how exact they have to be, the bound alone decides.
A program may use at most 64 MiB of HBM per device.

v0:
```python
import functools

import jax
import jax.numpy as jnp
import numpy as np
from jax import lax
from jax.experimental import pallas as pl
from jax.experimental.pallas import tpu as pltpu
from jax.sharding import PartitionSpec as P

S = 8
RHS = 8
STEPS = S + 1
COLS = RHS * STEPS
VMEM = pltpu.VMEM
MESH = pl.DeviceIdType.MESH
HIGHEST = lax.Precision.HIGHEST

viscosity = 0.04
diffusivity = 0.04
coupling = 0.5
spectral_shift = 0.5

SHIFT = -(6.0 * viscosity + spectral_shift)
BACK = 0.2


def change_of_basis():
    hessenberg = np.zeros((STEPS, STEPS))
    for k in range(STEPS):
        hessenberg[k, k] = SHIFT
        if k + 1 < STEPS:
            hessenberg[k + 1, k] = 1.0
        if k > 0:
            hessenberg[k - 1, k] = -BACK
    change = np.zeros((STEPS, STEPS))
    column = np.zeros(STEPS)
    column[0] = 1.0
    for k in range(STEPS):
        change[:, k] = column
        column = hessenberg @ column
    return change


def place(order):
    source, k = divmod(order, STEPS)
    return k * RHS + source


def output_constants():
    change = change_of_basis()
    permute = np.zeros((COLS, COLS), np.float32)
    mix = np.zeros((COLS, COLS), np.float32)
    for i in range(COLS):
        permute[i, place(i)] = 1.0
    for r in range(RHS):
        for a in range(STEPS):
            for b in range(STEPS):
                mix[a * RHS + r, r * STEPS + b] = change[a, b]
    return permute, mix


def split3(value):
    high = value.astype(jnp.bfloat16)
    rest = value - high.astype(jnp.float32)
    middle = rest.astype(jnp.bfloat16)
    low = (rest - middle.astype(jnp.float32)).astype(jnp.bfloat16)
    return high, middle, low


def basis_kernel(
    counts, cells,
    mask_ref, forcing_ref, flow_ref, shear_ref,
    basis_ref, inverse_ref, factor_ref,
    fields, gram, one, two,
    send_x, recv_x, send_y, recv_y, send_one, recv_one, send_two, recv_two, save_sem,
):
    count_x, count_y = counts
    cells_x, cells_y = cells
    gx = lax.axis_index("gx")
    gy = lax.axis_index("gy")

    barrier = pltpu.get_barrier_semaphore()
    for step in range(1, count_x):
        pl.semaphore_signal(
            barrier, inc=1, device_id=(lax.rem(gx + step, count_x), gy), device_id_type=MESH
        )
    for step in range(1, count_y):
        pl.semaphore_signal(
            barrier, inc=1, device_id=(gx, lax.rem(gy + step, count_y)), device_id_type=MESH
        )

    zero = jnp.zeros((8, 128), jnp.float32)
    lane = lax.broadcasted_iota(jnp.int32, (8, 128), 1)
    first_lane, last_lane = lane == 0, lane == 127

    def clear(k, carry):
        @pl.when(gx == 0)
        def _():
            fields[k, :, 0] = jnp.zeros(fields.shape[1:2] + fields.shape[3:], jnp.float32)

        @pl.when(gx == count_x - 1)
        def _():
            fields[k, :, cells_x + 1] = jnp.zeros(
                fields.shape[1:2] + fields.shape[3:], jnp.float32
            )

        @pl.when(gy == 0)
        def _():
            fields[k, :, :, 0] = jnp.zeros(fields.shape[1:3] + fields.shape[4:], jnp.float32)

        @pl.when(gy == count_y - 1)
        def _():
            fields[k, :, :, cells_y + 1] = jnp.zeros(
                fields.shape[1:3] + fields.shape[4:], jnp.float32
            )

        return carry

    lax.fori_loop(1, STEPS, clear, 0)
    fields[0] = jnp.zeros(fields.shape[1:], jnp.float32)

    def start_row(i, carry):
        x, y = i // cells_y, lax.rem(i, cells_y)
        mask = mask_ref[pl.ds(i, RHS, stride=cells_x * cells_y), :].astype(jnp.float32)
        for f in range(4):
            where = f * cells_x * cells_y + i
            value = forcing_ref[pl.ds(where, RHS, stride=4 * cells_x * cells_y), :]
            fields[1, f, x + 1, y + 1] = value * mask
        return carry

    lax.fori_loop(0, cells_x * cells_y, start_row, 0)
    pl.semaphore_wait(barrier, count_x + count_y - 2)

    def halo(k, axis, up):
        side = 1 if up else 0
        if axis == 0:
            source = cells_x if up else 1
            target = 0 if up else cells_x + 1
            rows = pl.ds(1, cells_y)
            return pltpu.make_async_remote_copy(
                src_ref=fields.at[k, :, source, rows],
                dst_ref=fields.at[k, :, target, rows],
                send_sem=send_x.at[k, side],
                recv_sem=recv_x.at[k, side],
                device_id=(gx + 1 if up else gx - 1, gy),
                device_id_type=MESH,
            )
        source = cells_y if up else 1
        target = 0 if up else cells_y + 1
        rows = pl.ds(1, cells_x)
        return pltpu.make_async_remote_copy(
            src_ref=fields.at[k, :, rows, source],
            dst_ref=fields.at[k, :, rows, target],
            send_sem=send_y.at[k, side],
            recv_sem=recv_y.at[k, side],
            device_id=(gx, gy + 1 if up else gy - 1),
            device_id_type=MESH,
        )

    def at_sides(k, axis, what):
        me, count = (gx, count_x) if axis == 0 else (gy, count_y)
        for up in (True, False):
            sends = me < count - 1 if up else me > 0
            receives = me > 0 if up else me < count - 1

            @pl.when(receives if what == "recv" else sends)
            def _(up=up):
                copy = halo(k, axis, up)
                if what == "start":
                    copy.start()
                elif what == "send":
                    copy.wait_send()
                else:
                    copy.wait_recv()

    def advance(k, x, y):
        def value(f, dx=0, dy=0):
            return fields[k, f, x + 1 + dx, y + 1 + dy]

        centre = [value(f) for f in range(4)]
        plus = [
            [value(f, 1, 0) for f in range(4)],
            [value(f, 0, 1) for f in range(4)],
            [jnp.where(last_lane, zero, pltpu.roll(centre[f], 127, 1)) for f in range(4)],
        ]
        minus = [
            [value(f, -1, 0) for f in range(4)],
            [value(f, 0, -1) for f in range(4)],
            [jnp.where(first_lane, zero, pltpu.roll(centre[f], 1, 1)) for f in range(4)],
        ]
        result = [BACK * fields[k - 1, f, x + 1, y + 1] for f in range(4)]
        for j in range(3):
            half = 0.5 * flow_ref[j, x, pl.ds(y, 1), :]
            ahead = jnp.broadcast_to(viscosity - half, (8, 128))
            behind = jnp.broadcast_to(viscosity + half, (8, 128))
            for i in range(3):
                result[i] = result[i] + ahead * plus[j][i] + behind * minus[j][i]
                shear = jnp.broadcast_to(shear_ref[i, j, x, pl.ds(y, 1), :], (8, 128))
                result[i] = result[i] - shear * centre[j]
            result[j] = result[j] - 0.5 * (plus[j][3] - minus[j][3])
            result[3] = result[3] + diffusivity * (plus[j][3] + minus[j][3])
            result[3] = result[3] - (0.5 * coupling) * (plus[j][j] - minus[j][j])
        for f in range(4):
            fields[k + 1, f, x + 1, y + 1] = result[f]

    def save(k):
        return pltpu.make_async_copy(
            fields.at[k, :, pl.ds(1, cells_x), pl.ds(1, cells_y)],
            basis_ref.at[:, :, :, pl.ds(pl.multiple_of((k - 1) * RHS, RHS), RHS)],
            save_sem.at[k],
        )

    def section(k, carry):
        def x_faces(y, carry):
            advance(k, 0, y)
            advance(k, cells_x - 1, y)
            return carry

        def y_faces(x, carry):
            advance(k, x, 0)
            advance(k, x, cells_y - 1)
            return carry

        def inside(y, carry):
            for x in range(1, cells_x - 1):
                advance(k, x, y)
            return carry

        at_sides(k, 0, "recv")
        at_sides(k, 1, "recv")
        lax.fori_loop(0, cells_y, x_faces, 0)

        @pl.when(k < S)
        def _():
            at_sides(k + 1, 0, "start")

        lax.fori_loop(1, cells_x - 1, y_faces, 0)

        @pl.when(k < S)
        def _():
            at_sides(k + 1, 1, "start")

        lax.fori_loop(1, cells_y - 1, inside, 0)
        save(k + 1).start()
        return carry

    at_sides(1, 0, "start")
    at_sides(1, 1, "start")
    save(1).start()
    lax.fori_loop(1, STEPS, section, 0)

    gram[...] = jnp.zeros_like(gram)
    padding = jnp.zeros((8, 128 * cells_y), jnp.float32)

    def accumulate(i, carry):
        f, x = i // cells_x, lax.rem(i, cells_x)
        block = jnp.concatenate(
            [
                jnp.concatenate([fields[k, f, x + 1, y + 1] for y in range(cells_y)], axis=1)
                for k in range(1, STEPS + 1)
            ]
            + [padding],
            axis=0,
        )
        parts = jnp.concatenate(split3(block), axis=0)
        gram[...] += lax.dot_general(
            parts, parts, (((1,), (1,)), ((), ())), preferred_element_type=jnp.float32
        )
        return carry

    lax.fori_loop(0, 4 * cells_x, accumulate, 0)
    height = COLS + 8
    own = gram[0:COLS, 0:COLS]
    for a in range(3):
        for b in range(3):
            if a or b:
                own = own + gram[a * height : a * height + COLS, b * height : b * height + COLS]
    own = jnp.concatenate([own, jnp.zeros((COLS, 128 - COLS), jnp.float32)], axis=1)

    def exchange(slots, me, count, device, send, recv):
        def copy(step, slot, partner):
            return pltpu.make_async_remote_copy(
                src_ref=slots.at[slot],
                dst_ref=slots.at[slot],
                send_sem=send.at[step],
                recv_sem=recv.at[step],
                device_id=device(partner),
                device_id_type=MESH,
            )

        for step in range(1, count):
            copy(step, me, lax.rem(me + step, count)).start()
        for step in range(1, count):
            source = lax.rem(me + count - step, count)
            copy(step, source, source).wait_recv()
        total = slots[0]
        for slot in range(1, count):
            total = total + slots[slot]
        for step in range(1, count):
            copy(step, me, lax.rem(me + step, count)).wait_send()
        return total

    one[gy] = own
    own = exchange(one, gy, count_y, lambda p: (gx, p), send_one, recv_one)
    two[gx] = own
    matrix = exchange(two, gx, count_x, lambda p: (p, gy), send_two, recv_two)

    rows = lax.broadcasted_iota(jnp.int32, (COLS, 128), 0)
    columns = lax.broadcasted_iota(jnp.int32, (COLS, 128), 1)
    rank = lax.rem(rows, RHS) * STEPS + rows // RHS
    column_rank = lax.rem(columns, RHS) * STEPS + columns // RHS
    inverse = jnp.where(rows == columns, 1.0, 0.0)
    for order in range(COLS):
        p = place(order)
        row = matrix[p : p + 1, :]
        inverse_row = inverse[p : p + 1, :]
        pivot = matrix[p : p + 1, p : p + 1]
        scale = lax.rsqrt(pivot)
        scale = scale * (1.5 - 0.5 * pivot * scale * scale)
        factor_ref[p : p + 1, :] = jnp.where(
            column_rank[0:1, :] >= order, row * scale, 0.0
        )
        inverse_ref[p : p + 1, :] = inverse_row * scale
        if order + 1 < COLS:
            multiple = matrix[:, p : p + 1] * (1.0 / pivot)
            multiple = jnp.where(rank > order, multiple, 0.0)
            matrix = matrix - multiple * row
            inverse = inverse - multiple * inverse_row

    def finish(k, carry):
        at_sides(k, 0, "send")
        at_sides(k, 1, "send")
        return carry

    lax.fori_loop(1, STEPS, finish, 0)
    for k in range(1, STEPS + 1):
        save(k).wait()


def basis(mask, forcing, flow, shear, counts):
    _, cells_x, cells_y, _ = flow.shape
    cells = (cells_x, cells_y)
    grid_cells = cells_x * cells_y
    count_x, count_y = counts
    height = COLS + 8
    dma = pltpu.SemaphoreType.DMA
    return pl.pallas_call(
        functools.partial(basis_kernel, counts, cells),
        out_shape=(
            jax.ShapeDtypeStruct((4, cells_x, cells_y, COLS, 128), jnp.float32),
            jax.ShapeDtypeStruct((COLS, 128), jnp.float32),
            jax.ShapeDtypeStruct((COLS, 128), jnp.float32),
        ),
        in_specs=[pl.BlockSpec(memory_space=VMEM)] * 4,
        out_specs=(
            pl.BlockSpec(memory_space=pl.ANY),
            pl.BlockSpec(memory_space=VMEM),
            pl.BlockSpec(memory_space=VMEM),
        ),
        scratch_shapes=[
            VMEM((STEPS + 1, 4, cells_x + 2, cells_y + 2, RHS, 128), jnp.float32),
            VMEM((3 * height, 3 * height), jnp.float32),
            VMEM((count_y, COLS, 128), jnp.float32),
            VMEM((count_x, COLS, 128), jnp.float32),
            dma((STEPS, 2)),
            dma((STEPS, 2)),
            dma((STEPS, 2)),
            dma((STEPS, 2)),
            dma((count_y,)),
            dma((count_y,)),
            dma((count_x,)),
            dma((count_x,)),
            dma((STEPS + 1,)),
        ],
        compiler_params=pltpu.CompilerParams(
            collective_id=0, has_side_effects=True, vmem_limit_bytes=40 * 1024 * 1024
        ),
        name="basis",
    )(
        mask.reshape(RHS * grid_cells, 128),
        forcing.reshape(RHS * 4 * grid_cells, 128),
        flow,
        shear,
    )


def orthonormal_kernel(
    all_cells, cells_y,
    basis_ref, inverse_ref, factor_ref, permute_ref, mix_ref,
    q_ref, r_ref, rms_ref,
):
    @pl.when((pl.program_id(0) == 0) & (pl.program_id(1) == 0))
    def _():
        rows = jnp.dot(
            permute_ref[...], factor_ref[:, 0:COLS],
            precision=HIGHEST, preferred_element_type=jnp.float32,
        )
        factor = jnp.dot(
            rows, mix_ref[...], precision=HIGHEST, preferred_element_type=jnp.float32
        )
        r_ref[...] = factor
        rms_ref[...] = jnp.sqrt(jnp.sum(factor * factor, axis=0, keepdims=True) / all_cells)

    block = jnp.concatenate([basis_ref[0, 0, y] for y in range(cells_y)], axis=1)
    result = jnp.dot(
        inverse_ref[:, 0:COLS], block, precision=HIGHEST, preferred_element_type=jnp.float32
    )
    q_rows = q_ref.reshape(COLS * cells_y, 128)
    for y in range(cells_y):
        for k in range(STEPS):
            q_rows[pl.ds(k * cells_y + y, RHS, stride=STEPS * cells_y), :] = result[
                k * RHS : (k + 1) * RHS, y * 128 : (y + 1) * 128
            ]


def orthonormal(all_cells, basis_rows, inverse, factor):
    fields, cells_x, cells_y, _, _ = basis_rows.shape
    permute, mix = output_constants()
    whole = lambda *shape: pl.BlockSpec(shape, lambda f, x: (0,) * len(shape))
    return pl.pallas_call(
        functools.partial(orthonormal_kernel, all_cells, cells_y),
        grid=(fields, cells_x),
        out_shape=(
            jax.ShapeDtypeStruct((COLS, fields, cells_x, cells_y, 128), jnp.float32),
            jax.ShapeDtypeStruct((COLS, COLS), jnp.float32),
            jax.ShapeDtypeStruct((1, COLS), jnp.float32),
        ),
        in_specs=[
            pl.BlockSpec((1, 1, cells_y, COLS, 128), lambda f, x: (f, x, 0, 0, 0)),
            whole(COLS, 128),
            whole(COLS, 128),
            whole(COLS, COLS),
            whole(COLS, COLS),
        ],
        out_specs=(
            pl.BlockSpec((COLS, 1, 1, cells_y, 128), lambda f, x: (0, f, x, 0, 0)),
            whole(COLS, COLS),
            whole(1, COLS),
        ),
        compiler_params=pltpu.CompilerParams(vmem_limit_bytes=24 * 1024 * 1024),
        name="orthonormal",
    )(basis_rows, inverse, factor, jnp.asarray(permute), jnp.asarray(mix))


def shards(actuator_mask, forcing, base_flow, base_shear):
    _, cells_x, cells_y, cells_z = base_flow.shape
    counts = (lax.axis_size("gx"), lax.axis_size("gy"))
    all_cells = 4.0 * cells_x * counts[0] * cells_y * counts[1] * cells_z
    rows, inverse, factor = basis(actuator_mask, forcing, base_flow, base_shear, counts)
    q_basis, r_factor, rms = orthonormal(all_cells, rows, inverse, factor)
    return (q_basis, r_factor, rms[0])


def solution(mesh):
    return jax.shard_map(
        shards,
        mesh=mesh,
        in_specs=(
            P(None, "gx", "gy", None),
            P(None, None, "gx", "gy", None),
            P(None, "gx", "gy", None),
            P(None, None, "gx", "gy", None),
        ),
        out_specs=(P(None, None, "gx", "gy", None), P(), P()),
        check_vma=False,
    )
```

profile of v0, /device:TPU:13, one launch (start us, length us, event | category | flops | bytes accessed | tf_op | source)
XLA Modules:
  0.0 105.3 jit_solution(1960475498362002825)
XLA Ops:
  0.6 0.0 copy-start
  0.6 1.0 copy-done
  1.7 0.0 copy-start.1
  1.7 0.9 copy-done.1
  2.6 0.0 copy-start.2
  2.6 0.9 copy-done.2
  3.5 0.0 copy-start.3
  3.5 0.8 copy-done.3
  4.3 89.7 %basis.1 = (f32[4,4,8,72,128]{4,3,2,1,0:T(8,128)S(1)}, f32[72,128]{1,0:T(8,128)S(1)}, f32[72,128]{1,0:T(8,128)S(1)}) custom-call(s32[256,128]{1,0:T(8,128)S(1)} %bitcast.4, f32[1024,128]{1,0:T(8,128)S(1)} %bitcast.3, f32[3,4,8,128]{3,2,1,0:T(8,128)S(1)} %copy-done.3, f32[3,3,4,8,128]{4,3,2,1,0:T(8,128)S(1)} %copy-done.1), custom_call_target="tpu_custom_call" | custom-call | tf_op jit(solution)/shard_map/basis/pallas_call | solution.py:348
  94.0 0.0 copy-start.4
  94.0 0.8 copy-done.4
  94.8 0.0 copy-start.5
  94.8 0.8 copy-done.5
  95.5 9.8 %orthonormal.1 = (f32[72,4,4,8,128]{4,3,2,1,0:T(8,128)}, f32[72,72]{1,0:T(8,128)}, f32[1,72]{1,0:T(1,128)}) custom-call(f32[4,4,8,72,128]{4,3,2,1,0:T(8,128)S(1)} %get-tuple-element.9.basis_ref, f32[72,128]{1,0:T(8,128)S(1)} %get-tuple-element.10.inverse_ref, f32[72,128]{1,0:T(8,128)S(1)} %get-tuple-element.11.factor_ref, f32[72,72]{1,0:T(8,128)S(1)} %copy-done.5, ...), custom_call_target="tpu_custom_call" | custom-call | tf_op jit(solution)/shard_map/orthonormal/pallas_call | solution.py:421
Async XLA Ops:
  0.6 1.0 copy-start
  1.7 0.9 copy-start.1
  2.6 0.9 copy-start.2
  3.5 0.8 copy-start.3
  94.0 0.8 copy-start.4
  94.8 0.8 copy-start.5
where the time goes:
time: 106 us; the launch traced here: 105 us
  Pallas kernels  99.5 us (94%)
  local copies, waits for them, and re-layouts  5.18 us (5%)
    pallas_call x1, Pallas kernels, basis(): pl.pallas_call(functools.partial(basis_kernel, counts, cells), out_shape=...  89.7 us
    pallas_call x1, Pallas kernels, orthonormal(): pl.pallas_call(functools.partial(orthonormal_kernel, all_cells, cells_y),...  9.81 us
    unnamed x12, local copies, waits for them, and re-layouts  5.18 us

commit v1 on v0

--- a/solution.py
+++ b/solution.py
@@ -12,6 +12,8 @@
 RHS = 8
 STEPS = S + 1
 COLS = RHS * STEPS
+PAIRS = (STEPS + 1) // 2
+PAIR = 48
 VMEM = pltpu.VMEM
 MESH = pl.DeviceIdType.MESH
 HIGHEST = lax.Precision.HIGHEST
@@ -70,15 +72,24 @@
 
 def basis_kernel(
     counts, cells,
-    mask_ref, forcing_ref, flow_ref, shear_ref,
-    basis_ref, inverse_ref, factor_ref,
-    fields, gram, one, two,
-    send_x, recv_x, send_y, recv_y, send_one, recv_one, send_two, recv_two, save_sem,
+    mask_hbm, forcing_hbm, flow_hbm, shear_hbm,
+    parts, inverse_ref, factor_ref,
+    mask_ref, forcing_ref, flow_ref, shear_ref, fields, gram, one, two,
+    send_x, recv_x, send_y, recv_y, send_one, recv_one, send_two, recv_two, load_sem,
 ):
     count_x, count_y = counts
     cells_x, cells_y = cells
     gx = lax.axis_index("gx")
     gy = lax.axis_index("gy")
+
+    arrays = (
+        (forcing_hbm, forcing_ref), (mask_hbm, mask_ref),
+        (flow_hbm, flow_ref), (shear_hbm, shear_ref),
+    )
+    loads = [pltpu.make_async_copy(a, b, load_sem.at[n]) for n, (a, b) in enumerate(arrays)]
+    for copy in loads:
+        copy.start()
+    early, late = loads[:2], loads[2:]
 
     barrier = pltpu.get_barrier_semaphore()
     for step in range(1, count_x):
@@ -129,6 +140,8 @@
             fields[1, f, x + 1, y + 1] = value * mask
         return carry
 
+    for copy in early:
+        copy.wait()
     lax.fori_loop(0, cells_x * cells_y, start_row, 0)
     pl.semaphore_wait(barrier, count_x + count_y - 2)
 
@@ -204,14 +217,24 @@
         for f in range(4):
             fields[k + 1, f, x + 1, y + 1] = result[f]
 
-    def save(k):
-        return pltpu.make_async_copy(
-            fields.at[k, :, pl.ds(1, cells_x), pl.ds(1, cells_y)],
-            basis_ref.at[:, :, :, pl.ds(pl.multiple_of((k - 1) * RHS, RHS), RHS)],
-            save_sem.at[k],
+    def inner_products(pair, i, second=True):
+        f, x = i // cells_x, lax.rem(i, cells_x)
+        k = 2 * pair + 1
+        first = jnp.concatenate([fields[k, f, x + 1, y + 1] for y in range(cells_y)], axis=1)
+        if second:
+            other = jnp.concatenate(
+                [fields[k + 1, f, x + 1, y + 1] for y in range(cells_y)], axis=1
+            )
+        else:
+            other = jnp.zeros_like(first)
+        new = jnp.concatenate(split3(jnp.concatenate([first, other], axis=0)), axis=0)
+        where = pl.ds(PAIR * pair if isinstance(pair, int) else pl.multiple_of(PAIR * pair, 16), PAIR)
+        parts[i, where, :] = new
+        gram[pair] += lax.dot_general(
+            parts[i], new, (((1,), (1,)), ((), ())), preferred_element_type=jnp.float32
         )
 
-    def section(k, carry):
+    def section(k):
         def x_faces(y, carry):
             advance(k, 0, y)
             advance(k, cells_x - 1, y)
@@ -242,41 +265,48 @@
             at_sides(k + 1, 1, "start")
 
         lax.fori_loop(1, cells_y - 1, inside, 0)
-        save(k + 1).start()
-        return carry
 
     at_sides(1, 0, "start")
     at_sides(1, 1, "start")
-    save(1).start()
-    lax.fori_loop(1, STEPS, section, 0)
-
     gram[...] = jnp.zeros_like(gram)
-    padding = jnp.zeros((8, 128 * cells_y), jnp.float32)
-
-    def accumulate(i, carry):
-        f, x = i // cells_x, lax.rem(i, cells_x)
-        block = jnp.concatenate(
-            [
-                jnp.concatenate([fields[k, f, x + 1, y + 1] for y in range(cells_y)], axis=1)
-                for k in range(1, STEPS + 1)
-            ]
-            + [padding],
-            axis=0,
-        )
-        parts = jnp.concatenate(split3(block), axis=0)
-        gram[...] += lax.dot_general(
-            parts, parts, (((1,), (1,)), ((), ())), preferred_element_type=jnp.float32
-        )
+    parts[...] = jnp.zeros_like(parts)
+    for copy in late:
+        copy.wait()
+    blocks = 4 * cells_x
+
+    def two_sections(pair, carry):
+        def products(i, carry):
+            inner_products(pair, i)
+            return carry
+
+        section(2 * pair + 1)
+        lax.fori_loop(0, blocks // 2, products, 0)
+        section(2 * pair + 2)
+        lax.fori_loop(blocks // 2, blocks, products, 0)
         return carry
 
-    lax.fori_loop(0, 4 * cells_x, accumulate, 0)
-    height = COLS + 8
-    own = gram[0:COLS, 0:COLS]
-    for a in range(3):
-        for b in range(3):
-            if a or b:
-                own = own + gram[a * height : a * height + COLS, b * height : b * height + COLS]
-    own = jnp.concatenate([own, jnp.zeros((COLS, 128 - COLS), jnp.float32)], axis=1)
+    lax.fori_loop(0, S // 2, two_sections, 0)
+
+    def last_products(i, carry):
+        inner_products(S // 2, i, second=False)
+        return carry
+
+    lax.fori_loop(0, blocks, last_products, 0)
+
+    pieces = []
+    for pair in range(PAIRS):
+        block = gram[pair]
+        block = block[:, 0:16] + block[:, 16:32] + block[:, 32:48]
+        tall = [
+            block[PAIR * a : PAIR * a + 16]
+            + block[PAIR * a + 16 : PAIR * a + 32]
+            + block[PAIR * a + 32 : PAIR * a + 48]
+            for a in range(pair + 1)
+        ]
+        tall = tall + [jnp.zeros((16 * (PAIRS - 1 - pair), 16), jnp.float32)] * (pair + 1 < PAIRS)
+        pieces.append(jnp.concatenate(tall, axis=0))
+    pieces.append(jnp.zeros((16 * PAIRS, 128 - 16 * PAIRS), jnp.float32))
+    own = jnp.concatenate(pieces, axis=1)[0:COLS]
 
     def exchange(slots, me, count, device, send, recv):
         def copy(step, slot, partner):
@@ -308,25 +338,38 @@
 
     rows = lax.broadcasted_iota(jnp.int32, (COLS, 128), 0)
     columns = lax.broadcasted_iota(jnp.int32, (COLS, 128), 1)
+    square = jnp.concatenate([matrix, jnp.zeros((128 - COLS, 128), jnp.float32)], axis=0)
+    mirror = jnp.transpose(square)[0:COLS]
+    matrix = jnp.where(rows // 16 <= columns // 16, matrix, mirror)
+
     rank = lax.rem(rows, RHS) * STEPS + rows // RHS
     column_rank = lax.rem(columns, RHS) * STEPS + columns // RHS
     inverse = jnp.where(rows == columns, 1.0, 0.0)
-    for order in range(COLS):
-        p = place(order)
-        row = matrix[p : p + 1, :]
-        inverse_row = inverse[p : p + 1, :]
-        pivot = matrix[p : p + 1, p : p + 1]
-        scale = lax.rsqrt(pivot)
-        scale = scale * (1.5 - 0.5 * pivot * scale * scale)
-        factor_ref[p : p + 1, :] = jnp.where(
-            column_rank[0:1, :] >= order, row * scale, 0.0
-        )
-        inverse_ref[p : p + 1, :] = inverse_row * scale
-        if order + 1 < COLS:
-            multiple = matrix[:, p : p + 1] * (1.0 / pivot)
-            multiple = jnp.where(rank > order, multiple, 0.0)
-            matrix = matrix - multiple * row
-            inverse = inverse - multiple * inverse_row
+    for source in range(RHS):
+        places = [k * RHS + source for k in range(STEPS)]
+        spread = [jnp.broadcast_to(matrix[:, p : p + 1], (COLS, 128)) for p in places]
+        for k, p in enumerate(places):
+            order = source * STEPS + k
+            row = matrix[p : p + 1, :]
+            inverse_row = inverse[p : p + 1, :]
+            pivot = spread[k][p : p + 1, :]
+            guess = pl.reciprocal(pivot, approx=True)
+            guess = guess * (2.0 - pivot * guess)
+            over = guess * (2.0 - pivot * guess)
+            scale = lax.rsqrt(pivot)
+            scale = scale * (1.5 - 0.5 * pivot * scale * scale)
+            factor_ref[p : p + 1, :] = jnp.where(
+                column_rank[0:1, :] >= order, row * scale, 0.0
+            )
+            inverse_ref[p : p + 1, :] = inverse_row * scale
+            if order + 1 < COLS:
+                multiple = jnp.where(rank > order, spread[k], 0.0)
+                matrix = matrix - multiple * (row * over)
+                inverse = inverse - multiple * (inverse_row * over)
+                for l in range(k + 1, STEPS):
+                    entry = spread[l][p : p + 1, :] * over
+                    spread[l] = spread[l] - multiple * entry
+    inverse_ref[COLS:, :] = jnp.zeros((16 * PAIRS - COLS, 128), jnp.float32)
 
     def finish(k, carry):
         at_sides(k, 0, "send")
@@ -334,8 +377,6 @@
         return carry
 
     lax.fori_loop(1, STEPS, finish, 0)
-    for k in range(1, STEPS + 1):
-        save(k).wait()
 
 
 def basis(mask, forcing, flow, shear, counts):
@@ -343,24 +384,24 @@
     cells = (cells_x, cells_y)
     grid_cells = cells_x * cells_y
     count_x, count_y = counts
-    height = COLS + 8
     dma = pltpu.SemaphoreType.DMA
+    height = 16 * PAIRS
     return pl.pallas_call(
         functools.partial(basis_kernel, counts, cells),
         out_shape=(
-            jax.ShapeDtypeStruct((4, cells_x, cells_y, COLS, 128), jnp.float32),
-            jax.ShapeDtypeStruct((COLS, 128), jnp.float32),
+            jax.ShapeDtypeStruct((4 * cells_x, PAIR * PAIRS, cells_y * 128), jnp.bfloat16),
+            jax.ShapeDtypeStruct((height, 128), jnp.float32),
             jax.ShapeDtypeStruct((COLS, 128), jnp.float32),
         ),
-        in_specs=[pl.BlockSpec(memory_space=VMEM)] * 4,
-        out_specs=(
-            pl.BlockSpec(memory_space=pl.ANY),
-            pl.BlockSpec(memory_space=VMEM),
-            pl.BlockSpec(memory_space=VMEM),
-        ),
+        in_specs=[pl.BlockSpec(memory_space=pltpu.HBM)] * 4,
+        out_specs=(pl.BlockSpec(memory_space=VMEM),) * 3,
         scratch_shapes=[
+            VMEM((RHS * grid_cells, 128), jnp.int32),
+            VMEM((RHS * 4 * grid_cells, 128), jnp.float32),
+            VMEM(flow.shape, jnp.float32),
+            VMEM(shear.shape, jnp.float32),
             VMEM((STEPS + 1, 4, cells_x + 2, cells_y + 2, RHS, 128), jnp.float32),
-            VMEM((3 * height, 3 * height), jnp.float32),
+            VMEM((PAIRS, PAIR * PAIRS, PAIR), jnp.float32),
             VMEM((count_y, COLS, 128), jnp.float32),
             VMEM((count_x, COLS, 128), jnp.float32),
             dma((STEPS, 2)),
@@ -371,7 +412,7 @@
             dma((count_y,)),
             dma((count_x,)),
             dma((count_x,)),
-            dma((STEPS + 1,)),
+            dma((4,)),
         ],
         compiler_params=pltpu.CompilerParams(
             collective_id=0, has_side_effects=True, vmem_limit_bytes=40 * 1024 * 1024
@@ -386,12 +427,44 @@
 
 
 def orthonormal_kernel(
-    all_cells, cells_y,
-    basis_ref, inverse_ref, factor_ref, permute_ref, mix_ref,
+    all_cells, cells_y, steps,
+    parts_ref, inverse_ref, factor_ref, permute_hbm, mix_hbm,
     q_ref, r_ref, rms_ref,
+    left, permute_ref, mix_ref, sem,
 ):
-    @pl.when((pl.program_id(0) == 0) & (pl.program_id(1) == 0))
+    step = pl.program_id(0)
+    height = 16 * PAIRS
+    loads = [
+        pltpu.make_async_copy(permute_hbm, permute_ref, sem.at[0]),
+        pltpu.make_async_copy(mix_hbm, mix_ref, sem.at[1]),
+    ]
+
+    @pl.when(step == 0)
     def _():
+        for copy in loads:
+            copy.start()
+        column = lax.broadcasted_iota(jnp.int32, (height, PAIR * PAIRS), 1)
+        row = lax.broadcasted_iota(jnp.int32, (height, PAIR * PAIRS), 0)
+        spread = jnp.where(
+            row == 16 * (column // PAIR) + lax.rem(column, 16), 1.0, 0.0
+        ).astype(jnp.bfloat16)
+        high, middle, _ = split3(inverse_ref[:, 0:height])
+        both = jnp.concatenate([high, middle], axis=0)
+        left[...] = jnp.dot(both, spread, preferred_element_type=jnp.float32).astype(jnp.bfloat16)
+
+    result = jnp.dot(left[...], parts_ref[0], preferred_element_type=jnp.float32)
+    result = result[0:COLS] + result[height : height + COLS]
+    q_rows = q_ref.reshape(COLS * cells_y, 128)
+    for y in range(cells_y):
+        for k in range(STEPS):
+            q_rows[pl.ds(k * cells_y + y, RHS, stride=STEPS * cells_y), :] = result[
+                k * RHS : (k + 1) * RHS, y * 128 : (y + 1) * 128
+            ]
+
+    @pl.when(step == steps - 1)
+    def _():
+        for copy in loads:
+            copy.wait()
         rows = jnp.dot(
             permute_ref[...], factor_ref[:, 0:COLS],
             precision=HIGHEST, preferred_element_type=jnp.float32,
@@ -402,45 +475,42 @@
         r_ref[...] = factor
         rms_ref[...] = jnp.sqrt(jnp.sum(factor * factor, axis=0, keepdims=True) / all_cells)
 
-    block = jnp.concatenate([basis_ref[0, 0, y] for y in range(cells_y)], axis=1)
-    result = jnp.dot(
-        inverse_ref[:, 0:COLS], block, precision=HIGHEST, preferred_element_type=jnp.float32
-    )
-    q_rows = q_ref.reshape(COLS * cells_y, 128)
-    for y in range(cells_y):
-        for k in range(STEPS):
-            q_rows[pl.ds(k * cells_y + y, RHS, stride=STEPS * cells_y), :] = result[
-                k * RHS : (k + 1) * RHS, y * 128 : (y + 1) * 128
-            ]
-
-
-def orthonormal(all_cells, basis_rows, inverse, factor):
-    fields, cells_x, cells_y, _, _ = basis_rows.shape
+
+def orthonormal(all_cells, cells, parts, inverse, factor):
+    cells_x, cells_y = cells
+    steps, depth, width = parts.shape
+    height = 16 * PAIRS
     permute, mix = output_constants()
-    whole = lambda *shape: pl.BlockSpec(shape, lambda f, x: (0,) * len(shape))
+    whole = lambda *shape: pl.BlockSpec(shape, lambda i: (0,) * len(shape))
     return pl.pallas_call(
-        functools.partial(orthonormal_kernel, all_cells, cells_y),
-        grid=(fields, cells_x),
+        functools.partial(orthonormal_kernel, all_cells, cells_y, steps),
+        grid=(steps,),
         out_shape=(
-            jax.ShapeDtypeStruct((COLS, fields, cells_x, cells_y, 128), jnp.float32),
+            jax.ShapeDtypeStruct((COLS, steps, cells_y, 128), jnp.float32),
             jax.ShapeDtypeStruct((COLS, COLS), jnp.float32),
             jax.ShapeDtypeStruct((1, COLS), jnp.float32),
         ),
         in_specs=[
-            pl.BlockSpec((1, 1, cells_y, COLS, 128), lambda f, x: (f, x, 0, 0, 0)),
+            pl.BlockSpec((1, depth, width), lambda i: (i, 0, 0)),
+            whole(height, 128),
             whole(COLS, 128),
-            whole(COLS, 128),
-            whole(COLS, COLS),
-            whole(COLS, COLS),
+            pl.BlockSpec(memory_space=pltpu.HBM),
+            pl.BlockSpec(memory_space=pltpu.HBM),
         ],
         out_specs=(
-            pl.BlockSpec((COLS, 1, 1, cells_y, 128), lambda f, x: (0, f, x, 0, 0)),
+            pl.BlockSpec((COLS, 1, cells_y, 128), lambda i: (0, i, 0, 0)),
             whole(COLS, COLS),
             whole(1, COLS),
         ),
+        scratch_shapes=[
+            VMEM((2 * height, depth), jnp.bfloat16),
+            VMEM((COLS, COLS), jnp.float32),
+            VMEM((COLS, COLS), jnp.float32),
+            pltpu.SemaphoreType.DMA((2,)),
+        ],
         compiler_params=pltpu.CompilerParams(vmem_limit_bytes=24 * 1024 * 1024),
         name="orthonormal",
-    )(basis_rows, inverse, factor, jnp.asarray(permute), jnp.asarray(mix))
+    )(parts, inverse, factor, jnp.asarray(permute), jnp.asarray(mix))
 
 
 def shards(actuator_mask, forcing, base_flow, base_shear):
@@ -448,8 +518,8 @@
     counts = (lax.axis_size("gx"), lax.axis_size("gy"))
     all_cells = 4.0 * cells_x * counts[0] * cells_y * counts[1] * cells_z
     rows, inverse, factor = basis(actuator_mask, forcing, base_flow, base_shear, counts)
-    q_basis, r_factor, rms = orthonormal(all_cells, rows, inverse, factor)
-    return (q_basis, r_factor, rms[0])
+    q_basis, r_factor, rms = orthonormal(all_cells, (cells_x, cells_y), rows, inverse, factor)
+    return (q_basis.reshape(COLS, 4, cells_x, cells_y, cells_z), r_factor, rms[0])
 
 
 def solution(mesh):

time: 106 us -> 103 us (0.972)
  the two profiles are of different devices: /device:TPU:13 before, /device:TPU:0 now
where the time goes in v1:
time: 103 us
  Pallas kernels  96.7 us (94%)
  local copies, waits for them, and re-layouts  5.18 us (5%)
    pallas_call x1, Pallas kernels, basis(): pl.pallas_call(functools.partial(basis_kernel, counts, cells), out_shape=...  88 us
    pallas_call x1, Pallas kernels, orthonormal(): pl.pallas_call(functools.partial(orthonormal_kernel, all_cells, cells_y,...  8.68 us
    unnamed x12, local copies, waits for them, and re-layouts  5.18 us

profile of v1, /device:TPU:0, one launch (start us, length us, event | category | flops | bytes accessed | tf_op | source)
XLA Modules:
  0.0 102.5 jit_solution(2075559459618858752)
XLA Ops:
  0.6 0.0 copy-start
  0.6 1.0 %copy-done = f32[8,4,4,8,128]{4,3,2,1,0:T(8,128)S(1)} copy-done((f32[8,4,4,8,128]{4,3,2,1,0:T(8,128)S(1)}, f32[8,4,4,8,128]{4,3,2,1,0:T(8,128)}, u32[]{:S(2)}) %copy-start) | copy-done | bytes 524312
  1.7 0.0 copy-start.1
  1.7 0.9 copy-done.1
  2.6 0.0 copy-start.2
  2.6 0.9 copy-done.2
  3.5 0.0 copy-start.3
  3.5 0.8 copy-done.3
  4.3 88.0 %basis.1 = (bf16[16,240,1024]{2,1,0:T(8,128)(2,1)S(1)}, f32[80,128]{1,0:T(8,128)S(1)}, f32[72,128]{1,0:T(8,128)S(1)}) custom-call(s32[256,128]{1,0:T(8,128)S(1)} %bitcast.5, f32[1024,128]{1,0:T(8,128)S(1)} %bitcast.4, f32[3,4,8,128]{3,2,1,0:T(8,128)S(1)} %copy-done.3, f32[3,3,4,8,128]{4,3,2,1,0:T(8,128)S(1)} %copy-done.1), custom_call_target="tpu_custom_call" | custom-call | tf_op jit(solution)/shard_map/basis/pallas_call | solution.py:389
  92.3 0.0 copy-start.4
  92.3 0.8 copy-done.4
  93.1 0.0 copy-start.5
  93.1 0.8 copy-done.5
  93.9 8.7 %orthonormal.1 = (f32[72,16,8,128]{3,2,1,0:T(8,128)}, f32[72,72]{1,0:T(8,128)}, f32[1,72]{1,0:T(1,128)}) custom-call(bf16[16,240,1024]{2,1,0:T(8,128)(2,1)S(1)} %get-tuple-element.9.parts_ref, f32[80,128]{1,0:T(8,128)S(1)} %get-tuple-element.10.inverse_ref, f32[72,128]{1,0:T(8,128)S(1)} %get-tuple-element.11.factor_ref, f32[72,72]{1,0:T(8,128)S(1)} %copy-done.5, ...), custom_call_target="tpu_custom_call" | custom-call | tf_op jit(solution)/shard_map/orthonormal/pallas_call | solution.py:485
Async XLA Ops:
  0.6 1.0 %copy-start = (f32[8,4,4,8,128]{4,3,2,1,0:T(8,128)S(1)}, f32[8,4,4,8,128]{4,3,2,1,0:T(8,128)}, u32[]{:S(2)}) copy-start(f32[8,4,4,8,128]{4,3,2,1,0:T(8,128)} %param.7) | copy-start | bytes 1572868
  1.7 0.9 copy-start.1
  2.6 0.9 copy-start.2
  3.5 0.8 copy-start.3
  92.3 0.8 copy-start.4
  93.1 0.8 copy-start.5

commit v2 on v1

--- a/solution.py
+++ b/solution.py
@@ -14,6 +14,7 @@
 COLS = RHS * STEPS
 PAIRS = (STEPS + 1) // 2
 PAIR = 48
+PIECES = 4
 VMEM = pltpu.VMEM
 MESH = pl.DeviceIdType.MESH
 HIGHEST = lax.Precision.HIGHEST
@@ -49,17 +50,25 @@
     return k * RHS + source
 
 
-def output_constants():
+def permutation(height, width):
+    rows = lax.broadcasted_iota(jnp.int32, (height, width), 0)
+    columns = lax.broadcasted_iota(jnp.int32, (height, width), 1)
+    places = lax.rem(rows, STEPS) * RHS + rows // STEPS
+    return jnp.where((places == columns) & (rows < COLS), 1.0, 0.0)
+
+
+def mixing():
     change = change_of_basis()
-    permute = np.zeros((COLS, COLS), np.float32)
-    mix = np.zeros((COLS, COLS), np.float32)
-    for i in range(COLS):
-        permute[i, place(i)] = 1.0
-    for r in range(RHS):
-        for a in range(STEPS):
-            for b in range(STEPS):
-                mix[a * RHS + r, r * STEPS + b] = change[a, b]
-    return permute, mix
+    rows = lax.broadcasted_iota(jnp.int32, (COLS, COLS), 0)
+    columns = lax.broadcasted_iota(jnp.int32, (COLS, COLS), 1)
+    degree = jnp.where(
+        lax.rem(rows, RHS) == columns // STEPS, STEPS * (rows // RHS) + lax.rem(columns, STEPS), -1
+    )
+    mix = jnp.zeros((COLS, COLS), jnp.float32)
+    for a in range(STEPS):
+        for b in range(a, STEPS):
+            mix = jnp.where(degree == STEPS * a + b, float(change[a, b]), mix)
+    return mix
 
 
 def split3(value):
@@ -73,12 +82,13 @@
 def basis_kernel(
     counts, cells,
     mask_hbm, forcing_hbm, flow_hbm, shear_hbm,
-    parts, inverse_ref, factor_ref,
-    mask_ref, forcing_ref, flow_ref, shear_ref, fields, gram, one, two,
-    send_x, recv_x, send_y, recv_y, send_one, recv_one, send_two, recv_two, load_sem,
+    parts_hbm, inverse_ref, factor_ref,
+    mask_ref, forcing_ref, flow_ref, shear_ref, parts, fields, gram, one, two,
+    send_x, recv_x, send_y, recv_y, send_one, recv_one, send_two, recv_two, load_sem, save_sem,
 ):
     count_x, count_y = counts
     cells_x, cells_y = cells
+    depth = cells_y // PIECES
     gx = lax.axis_index("gx")
     gy = lax.axis_index("gy")
 
@@ -145,17 +155,17 @@
     lax.fori_loop(0, cells_x * cells_y, start_row, 0)
     pl.semaphore_wait(barrier, count_x + count_y - 2)
 
-    def halo(k, axis, up):
+    def halo(k, axis, up, piece):
         side = 1 if up else 0
         if axis == 0:
             source = cells_x if up else 1
             target = 0 if up else cells_x + 1
-            rows = pl.ds(1, cells_y)
+            rows = pl.ds(1 + piece * depth, depth)
             return pltpu.make_async_remote_copy(
                 src_ref=fields.at[k, :, source, rows],
                 dst_ref=fields.at[k, :, target, rows],
-                send_sem=send_x.at[k, side],
-                recv_sem=recv_x.at[k, side],
+                send_sem=send_x.at[k, side, piece],
+                recv_sem=recv_x.at[k, side, piece],
                 device_id=(gx + 1 if up else gx - 1, gy),
                 device_id_type=MESH,
             )
@@ -171,7 +181,7 @@
             device_id_type=MESH,
         )
 
-    def at_sides(k, axis, what):
+    def at_sides(k, axis, what, piece=0):
         me, count = (gx, count_x) if axis == 0 else (gy, count_y)
         for up in (True, False):
             sends = me < count - 1 if up else me > 0
@@ -179,7 +189,7 @@
 
             @pl.when(receives if what == "recv" else sends)
             def _(up=up):
-                copy = halo(k, axis, up)
+                copy = halo(k, axis, up, piece)
                 if what == "start":
                     copy.start()
                 elif what == "send":
@@ -228,18 +238,13 @@
         else:
             other = jnp.zeros_like(first)
         new = jnp.concatenate(split3(jnp.concatenate([first, other], axis=0)), axis=0)
-        where = pl.ds(PAIR * pair if isinstance(pair, int) else pl.multiple_of(PAIR * pair, 16), PAIR)
-        parts[i, where, :] = new
-        gram[pair] += lax.dot_general(
-            parts[i], new, (((1,), (1,)), ((), ())), preferred_element_type=jnp.float32
+        parts[i, PAIR * pair : PAIR * (pair + 1), :] = new
+        below = slice(0, PAIR * (pair + 1))
+        gram[pair, below] += lax.dot_general(
+            parts[i, below], new, (((1,), (1,)), ((), ())), preferred_element_type=jnp.float32
         )
 
     def section(k):
-        def x_faces(y, carry):
-            advance(k, 0, y)
-            advance(k, cells_x - 1, y)
-            return carry
-
         def y_faces(x, carry):
             advance(k, x, 0)
             advance(k, x, cells_y - 1)
@@ -250,31 +255,35 @@
                 advance(k, x, y)
             return carry
 
-        at_sides(k, 0, "recv")
+        def piece_of_faces(piece, carry):
+            at_sides(k, 0, "recv", piece)
+            for y in range(depth):
+                advance(k, 0, piece * depth + y)
+                advance(k, cells_x - 1, piece * depth + y)
+
+            if k < S:
+                at_sides(k + 1, 0, "start", piece)
+
+            return carry
+
         at_sides(k, 1, "recv")
-        lax.fori_loop(0, cells_y, x_faces, 0)
-
-        @pl.when(k < S)
-        def _():
-            at_sides(k + 1, 0, "start")
-
+        lax.fori_loop(0, PIECES, piece_of_faces, 0)
         lax.fori_loop(1, cells_x - 1, y_faces, 0)
 
-        @pl.when(k < S)
-        def _():
+        if k < S:
             at_sides(k + 1, 1, "start")
 
         lax.fori_loop(1, cells_y - 1, inside, 0)
 
-    at_sides(1, 0, "start")
+    for piece in range(PIECES):
+        at_sides(1, 0, "start", piece)
     at_sides(1, 1, "start")
     gram[...] = jnp.zeros_like(gram)
-    parts[...] = jnp.zeros_like(parts)
     for copy in late:
         copy.wait()
     blocks = 4 * cells_x
 
-    def two_sections(pair, carry):
+    def two_sections(pair):
         def products(i, carry):
             inner_products(pair, i)
             return carry
@@ -283,15 +292,17 @@
         lax.fori_loop(0, blocks // 2, products, 0)
         section(2 * pair + 2)
         lax.fori_loop(blocks // 2, blocks, products, 0)
-        return carry
-
-    lax.fori_loop(0, S // 2, two_sections, 0)
+
+    for pair in range(S // 2):
+        two_sections(pair)
 
     def last_products(i, carry):
         inner_products(S // 2, i, second=False)
         return carry
 
     lax.fori_loop(0, blocks, last_products, 0)
+    save = pltpu.make_async_copy(parts, parts_hbm, save_sem)
+    save.start()
 
     pieces = []
     for pair in range(PAIRS):
@@ -372,11 +383,13 @@
     inverse_ref[COLS:, :] = jnp.zeros((16 * PAIRS - COLS, 128), jnp.float32)
 
     def finish(k, carry):
-        at_sides(k, 0, "send")
+        for piece in range(PIECES):
+            at_sides(k, 0, "send", piece)
         at_sides(k, 1, "send")
         return carry
 
     lax.fori_loop(1, STEPS, finish, 0)
+    save.wait()
 
 
 def basis(mask, forcing, flow, shear, counts):
@@ -394,18 +407,23 @@
             jax.ShapeDtypeStruct((COLS, 128), jnp.float32),
         ),
         in_specs=[pl.BlockSpec(memory_space=pltpu.HBM)] * 4,
-        out_specs=(pl.BlockSpec(memory_space=VMEM),) * 3,
+        out_specs=(
+            pl.BlockSpec(memory_space=pltpu.HBM),
+            pl.BlockSpec(memory_space=VMEM),
+            pl.BlockSpec(memory_space=VMEM),
+        ),
         scratch_shapes=[
             VMEM((RHS * grid_cells, 128), jnp.int32),
             VMEM((RHS * 4 * grid_cells, 128), jnp.float32),
             VMEM(flow.shape, jnp.float32),
             VMEM(shear.shape, jnp.float32),
+            VMEM((4 * cells_x, PAIR * PAIRS, cells_y * 128), jnp.bfloat16),
             VMEM((STEPS + 1, 4, cells_x + 2, cells_y + 2, RHS, 128), jnp.float32),
             VMEM((PAIRS, PAIR * PAIRS, PAIR), jnp.float32),
             VMEM((count_y, COLS, 128), jnp.float32),
             VMEM((count_x, COLS, 128), jnp.float32),
-            dma((STEPS, 2)),
-            dma((STEPS, 2)),
+            dma((STEPS, 2, PIECES)),
+            dma((STEPS, 2, PIECES)),
             dma((STEPS, 2)),
             dma((STEPS, 2)),
             dma((count_y,)),
@@ -413,9 +431,10 @@
             dma((count_x,)),
             dma((count_x,)),
             dma((4,)),
+            dma,
         ],
         compiler_params=pltpu.CompilerParams(
-            collective_id=0, has_side_effects=True, vmem_limit_bytes=40 * 1024 * 1024
+            collective_id=0, has_side_effects=True, vmem_limit_bytes=55 * 1024 * 1024
         ),
         name="basis",
     )(
@@ -428,49 +447,44 @@
 
 def orthonormal_kernel(
     all_cells, cells_y, steps,
-    parts_ref, inverse_ref, factor_ref, permute_hbm, mix_hbm,
+    parts_ref, inverse_ref, factor_ref,
     q_ref, r_ref, rms_ref,
-    left, permute_ref, mix_ref, sem,
+    left,
 ):
     step = pl.program_id(0)
     height = 16 * PAIRS
-    loads = [
-        pltpu.make_async_copy(permute_hbm, permute_ref, sem.at[0]),
-        pltpu.make_async_copy(mix_hbm, mix_ref, sem.at[1]),
-    ]
 
     @pl.when(step == 0)
     def _():
-        for copy in loads:
-            copy.start()
         column = lax.broadcasted_iota(jnp.int32, (height, PAIR * PAIRS), 1)
         row = lax.broadcasted_iota(jnp.int32, (height, PAIR * PAIRS), 0)
         spread = jnp.where(
             row == 16 * (column // PAIR) + lax.rem(column, 16), 1.0, 0.0
         ).astype(jnp.bfloat16)
         high, middle, _ = split3(inverse_ref[:, 0:height])
-        both = jnp.concatenate([high, middle], axis=0)
+        order = permutation(height, height).astype(jnp.bfloat16)
+        both = jnp.concatenate(
+            [
+                jnp.dot(order, part, preferred_element_type=jnp.float32).astype(jnp.bfloat16)
+                for part in (high, middle)
+            ],
+            axis=0,
+        )
         left[...] = jnp.dot(both, spread, preferred_element_type=jnp.float32).astype(jnp.bfloat16)
 
     result = jnp.dot(left[...], parts_ref[0], preferred_element_type=jnp.float32)
     result = result[0:COLS] + result[height : height + COLS]
-    q_rows = q_ref.reshape(COLS * cells_y, 128)
-    for y in range(cells_y):
-        for k in range(STEPS):
-            q_rows[pl.ds(k * cells_y + y, RHS, stride=STEPS * cells_y), :] = result[
-                k * RHS : (k + 1) * RHS, y * 128 : (y + 1) * 128
-            ]
+    planes = [result[:, y * 128 : (y + 1) * 128] for y in range(cells_y)]
+    q_ref[:, 0] = jnp.swapaxes(jnp.stack(planes, axis=0), 0, 1)
 
     @pl.when(step == steps - 1)
     def _():
-        for copy in loads:
-            copy.wait()
         rows = jnp.dot(
-            permute_ref[...], factor_ref[:, 0:COLS],
+            permutation(COLS, COLS), factor_ref[:, 0:COLS],
             precision=HIGHEST, preferred_element_type=jnp.float32,
         )
         factor = jnp.dot(
-            rows, mix_ref[...], precision=HIGHEST, preferred_element_type=jnp.float32
+            rows, mixing(), precision=HIGHEST, preferred_element_type=jnp.float32
         )
         r_ref[...] = factor
         rms_ref[...] = jnp.sqrt(jnp.sum(factor * factor, axis=0, keepdims=True) / all_cells)
@@ -480,7 +494,6 @@
     cells_x, cells_y = cells
     steps, depth, width = parts.shape
     height = 16 * PAIRS
-    permute, mix = output_constants()
     whole = lambda *shape: pl.BlockSpec(shape, lambda i: (0,) * len(shape))
     return pl.pallas_call(
         functools.partial(orthonormal_kernel, all_cells, cells_y, steps),
@@ -494,8 +507,6 @@
             pl.BlockSpec((1, depth, width), lambda i: (i, 0, 0)),
             whole(height, 128),
             whole(COLS, 128),
-            pl.BlockSpec(memory_space=pltpu.HBM),
-            pl.BlockSpec(memory_space=pltpu.HBM),
         ],
         out_specs=(
             pl.BlockSpec((COLS, 1, cells_y, 128), lambda i: (0, i, 0, 0)),
@@ -504,13 +515,10 @@
         ),
         scratch_shapes=[
             VMEM((2 * height, depth), jnp.bfloat16),
-            VMEM((COLS, COLS), jnp.float32),
-            VMEM((COLS, COLS), jnp.float32),
-            pltpu.SemaphoreType.DMA((2,)),
         ],
-        compiler_params=pltpu.CompilerParams(vmem_limit_bytes=24 * 1024 * 1024),
+        compiler_params=pltpu.CompilerParams(vmem_limit_bytes=55 * 1024 * 1024),
         name="orthonormal",
-    )(parts, inverse, factor, jnp.asarray(permute), jnp.asarray(mix))
+    )(parts, inverse, factor)
 
 
 def shards(actuator_mask, forcing, base_flow, base_shear):

time: 103 us -> 89.6 us (0.87)
  Pallas kernels: 96.7 us -> 88.5 us
  local copies, waits for them, and re-layouts: 5.18 us -> 0 us
    pallas_call x1, Pallas kernels: 88 us -> 75 us  [basis(): pl.pallas_call(functools.partial(basis_kernel, counts, cells), out_shape=...]
    unnamed x12 -> x0, local copies, waits for them, and re-layouts: 5.18 us -> none
    pallas_call x1, Pallas kernels: 8.68 us -> 13.5 us  [orthonormal(): pl.pallas_call(functools.partial(orthonormal_kernel, all_cells, cells_y,...]
where the time goes in v2:
time: 89.6 us; the launch traced here: 89.2 us
  Pallas kernels  88.5 us (99%)
    pallas_call x1, Pallas kernels, basis(): pl.pallas_call(functools.partial(basis_kernel, counts, cells), out_shape=...  75 us
    pallas_call x1, Pallas kernels, orthonormal(): pl.pallas_call(functools.partial(orthonormal_kernel, all_cells, cells_y,...  13.5 us

profile of v2, /device:TPU:0, one launch (start us, length us, event | category | flops | bytes accessed | tf_op | source)
XLA Modules:
  0.0 89.2 jit_solution(15867095279974282737)
XLA Ops:
  0.6 75.0 %basis.1 = (bf16[16,240,1024]{2,1,0:T(8,128)(2,1)}, f32[80,128]{1,0:T(8,128)}, f32[72,128]{1,0:T(8,128)}) custom-call(s32[256,128]{1,0:T(8,128)} %bitcast.5, f32[1024,128]{1,0:T(8,128)} %bitcast.4, f32[3,4,8,128]{3,2,1,0:T(8,128)} %flow_hbm.1, f32[3,3,4,8,128]{4,3,2,1,0:T(8,128)} %shear_hbm.1), custom_call_target="tpu_custom_call" | custom-call | tf_op jit(solution)/shard_map/basis/pallas_call | solution.py:402
  75.6 13.5 %orthonormal.1 = (f32[72,16,8,128]{3,2,1,0:T(8,128)}, f32[72,72]{1,0:T(8,128)}, f32[1,72]{1,0:T(1,128)}) custom-call(bf16[16,240,1024]{2,1,0:T(8,128)(2,1)} %get-tuple-element.9.parts_ref, f32[80,128]{1,0:T(8,128)} %get-tuple-element.10.inverse_ref, f32[72,128]{1,0:T(8,128)} %get-tuple-element.11.factor_ref), custom_call_target="tpu_custom_call" | custom-call | tf_op jit(solution)/shard_map/orthonormal/pallas_call | solution.py:498

commit v3 on v2

--- a/solution.py
+++ b/solution.py
@@ -13,8 +13,9 @@
 STEPS = S + 1
 COLS = RHS * STEPS
 PAIRS = (STEPS + 1) // 2
-PAIR = 48
+PAIR = 32
 PIECES = 4
+WIDTH = 128 * (-(-8 * PAIRS * (PAIRS + 1) // 128))
 VMEM = pltpu.VMEM
 MESH = pl.DeviceIdType.MESH
 HIGHEST = lax.Precision.HIGHEST
@@ -71,12 +72,9 @@
     return mix
 
 
-def split3(value):
+def split2(value):
     high = value.astype(jnp.bfloat16)
-    rest = value - high.astype(jnp.float32)
-    middle = rest.astype(jnp.bfloat16)
-    low = (rest - middle.astype(jnp.float32)).astype(jnp.bfloat16)
-    return high, middle, low
+    return high, (value - high.astype(jnp.float32)).astype(jnp.bfloat16)
 
 
 def basis_kernel(
@@ -237,7 +235,7 @@
             )
         else:
             other = jnp.zeros_like(first)
-        new = jnp.concatenate(split3(jnp.concatenate([first, other], axis=0)), axis=0)
+        new = jnp.concatenate(split2(jnp.concatenate([first, other], axis=0)), axis=0)
         parts[i, PAIR * pair : PAIR * (pair + 1), :] = new
         below = slice(0, PAIR * (pair + 1))
         gram[pair, below] += lax.dot_general(
@@ -307,17 +305,11 @@
     pieces = []
     for pair in range(PAIRS):
         block = gram[pair]
-        block = block[:, 0:16] + block[:, 16:32] + block[:, 32:48]
-        tall = [
-            block[PAIR * a : PAIR * a + 16]
-            + block[PAIR * a + 16 : PAIR * a + 32]
-            + block[PAIR * a + 32 : PAIR * a + 48]
-            for a in range(pair + 1)
-        ]
-        tall = tall + [jnp.zeros((16 * (PAIRS - 1 - pair), 16), jnp.float32)] * (pair + 1 < PAIRS)
-        pieces.append(jnp.concatenate(tall, axis=0))
-    pieces.append(jnp.zeros((16 * PAIRS, 128 - 16 * PAIRS), jnp.float32))
-    own = jnp.concatenate(pieces, axis=1)[0:COLS]
+        block = block[:, 0:16] + block[:, 16:32]
+        for a in range(pair + 1):
+            pieces.append(block[PAIR * a : PAIR * a + 16] + block[PAIR * a + 16 : PAIR * (a + 1)])
+    pieces.append(jnp.zeros((16, WIDTH - 16 * len(pieces)), jnp.float32))
+    own = jnp.concatenate(pieces, axis=1)
 
     def exchange(slots, me, count, device, send, recv):
         def copy(step, slot, partner):
@@ -345,11 +337,20 @@
     one[gy] = own
     own = exchange(one, gy, count_y, lambda p: (gx, p), send_one, recv_one)
     two[gx] = own
-    matrix = exchange(two, gx, count_x, lambda p: (p, gy), send_two, recv_two)
-
+    total = exchange(two, gx, count_x, lambda p: (p, gy), send_two, recv_two)
+
+    strips = []
+    for a in range(PAIRS):
+        spots = [pair * (pair + 1) // 2 + a for pair in range(a, PAIRS)]
+        strip = [total[:, 16 * spot : 16 * (spot + 1)] for spot in spots]
+        if a:
+            strip = [jnp.zeros((16, 16 * a), jnp.float32)] + strip
+        strip.append(jnp.zeros((16, 128 - 16 * PAIRS), jnp.float32))
+        strips.append(jnp.concatenate(strip, axis=1))
     rows = lax.broadcasted_iota(jnp.int32, (COLS, 128), 0)
     columns = lax.broadcasted_iota(jnp.int32, (COLS, 128), 1)
-    square = jnp.concatenate([matrix, jnp.zeros((128 - COLS, 128), jnp.float32)], axis=0)
+    square = jnp.concatenate(strips + [jnp.zeros((128 - 16 * PAIRS, 128), jnp.float32)], axis=0)
+    matrix = square[0:COLS]
     mirror = jnp.transpose(square)[0:COLS]
     matrix = jnp.where(rows // 16 <= columns // 16, matrix, mirror)
 
@@ -420,8 +421,8 @@
             VMEM((4 * cells_x, PAIR * PAIRS, cells_y * 128), jnp.bfloat16),
             VMEM((STEPS + 1, 4, cells_x + 2, cells_y + 2, RHS, 128), jnp.float32),
             VMEM((PAIRS, PAIR * PAIRS, PAIR), jnp.float32),
-            VMEM((count_y, COLS, 128), jnp.float32),
-            VMEM((count_x, COLS, 128), jnp.float32),
+            VMEM((count_y, 16, WIDTH), jnp.float32),
+            VMEM((count_x, 16, WIDTH), jnp.float32),
             dma((STEPS, 2, PIECES)),
             dma((STEPS, 2, PIECES)),
             dma((STEPS, 2)),
@@ -461,7 +462,7 @@
         spread = jnp.where(
             row == 16 * (column // PAIR) + lax.rem(column, 16), 1.0, 0.0
         ).astype(jnp.bfloat16)
-        high, middle, _ = split3(inverse_ref[:, 0:height])
+        high, middle = split2(inverse_ref[:, 0:height])
         order = permutation(height, height).astype(jnp.bfloat16)
         both = jnp.concatenate(
             [
@@ -474,8 +475,12 @@
 
     result = jnp.dot(left[...], parts_ref[0], preferred_element_type=jnp.float32)
     result = result[0:COLS] + result[height : height + COLS]
-    planes = [result[:, y * 128 : (y + 1) * 128] for y in range(cells_y)]
-    q_ref[:, 0] = jnp.swapaxes(jnp.stack(planes, axis=0), 0, 1)
+    q_rows = q_ref.reshape(COLS * cells_y, 128)
+    for y in range(cells_y):
+        for c in range(0, COLS, 8):
+            q_rows[pl.ds(c * cells_y + y, 8, stride=cells_y), :] = result[
+                c : c + 8, y * 128 : (y + 1) * 128
+            ]
 
     @pl.when(step == steps - 1)
     def _():

time: 89.6 us -> 85.4 us (0.953)
  Pallas kernels: 88.5 us -> 84.4 us
    pallas_call x1, Pallas kernels: 75 us -> 71.6 us  [basis(): pl.pallas_call(functools.partial(basis_kernel, counts, cells), out_shape=...]
where the time goes in v3:
time: 85.4 us; the launch traced here: 85 us
  Pallas kernels  84.4 us (99%)
    pallas_call x1, Pallas kernels, basis(): pl.pallas_call(functools.partial(basis_kernel, counts, cells), out_shape=...  71.6 us
    pallas_call x1, Pallas kernels, orthonormal(): pl.pallas_call(functools.partial(orthonormal_kernel, all_cells, cells_y,...  12.8 us

profile of v3, /device:TPU:0, one launch (start us, length us, event | category | flops | bytes accessed | tf_op | source)
XLA Modules:
  0.0 85.0 jit_solution(10769530274552165410)
XLA Ops:
  0.6 71.6 %basis.1 = (bf16[16,160,1024]{2,1,0:T(8,128)(2,1)}, f32[80,128]{1,0:T(8,128)}, f32[72,128]{1,0:T(8,128)}) custom-call(s32[256,128]{1,0:T(8,128)} %bitcast.5, f32[1024,128]{1,0:T(8,128)} %bitcast.4, f32[3,4,8,128]{3,2,1,0:T(8,128)} %flow_hbm.1, f32[3,3,4,8,128]{4,3,2,1,0:T(8,128)} %shear_hbm.1), custom_call_target="tpu_custom_call" | custom-call | tf_op jit(solution)/shard_map/basis/pallas_call | solution.py:403
  72.2 12.8 %orthonormal.1 = (f32[72,16,8,128]{3,2,1,0:T(8,128)}, f32[72,72]{1,0:T(8,128)}, f32[1,72]{1,0:T(1,128)}) custom-call(bf16[16,160,1024]{2,1,0:T(8,128)(2,1)} %get-tuple-element.9.parts_ref, f32[80,128]{1,0:T(8,128)} %get-tuple-element.10.inverse_ref, f32[72,128]{1,0:T(8,128)} %get-tuple-element.11.factor_ref), custom_call_target="tpu_custom_call" | custom-call | tf_op jit(solution)/shard_map/orthonormal/pallas_call | solution.py:503

commit v4 on v3

--- a/solution.py
+++ b/solution.py
@@ -447,79 +447,96 @@
 
 
 def orthonormal_kernel(
-    all_cells, cells_y, steps,
-    parts_ref, inverse_ref, factor_ref,
-    q_ref, r_ref, rms_ref,
-    left,
+    all_cells, cells_y, blocks, group,
+    parts_hbm, inverse_ref, factor_ref,
+    q_hbm, r_ref, rms_ref,
+    left, parts, q, load_sem, save_sem,
 ):
-    step = pl.program_id(0)
     height = 16 * PAIRS
 
-    @pl.when(step == 0)
-    def _():
-        column = lax.broadcasted_iota(jnp.int32, (height, PAIR * PAIRS), 1)
-        row = lax.broadcasted_iota(jnp.int32, (height, PAIR * PAIRS), 0)
-        spread = jnp.where(
-            row == 16 * (column // PAIR) + lax.rem(column, 16), 1.0, 0.0
-        ).astype(jnp.bfloat16)
-        high, middle = split2(inverse_ref[:, 0:height])
-        order = permutation(height, height).astype(jnp.bfloat16)
-        both = jnp.concatenate(
-            [
-                jnp.dot(order, part, preferred_element_type=jnp.float32).astype(jnp.bfloat16)
-                for part in (high, middle)
-            ],
-            axis=0,
-        )
-        left[...] = jnp.dot(both, spread, preferred_element_type=jnp.float32).astype(jnp.bfloat16)
-
-    result = jnp.dot(left[...], parts_ref[0], preferred_element_type=jnp.float32)
-    result = result[0:COLS] + result[height : height + COLS]
-    q_rows = q_ref.reshape(COLS * cells_y, 128)
-    for y in range(cells_y):
-        for c in range(0, COLS, 8):
-            q_rows[pl.ds(c * cells_y + y, 8, stride=cells_y), :] = result[
-                c : c + 8, y * 128 : (y + 1) * 128
-            ]
-
-    @pl.when(step == steps - 1)
-    def _():
-        rows = jnp.dot(
-            permutation(COLS, COLS), factor_ref[:, 0:COLS],
-            precision=HIGHEST, preferred_element_type=jnp.float32,
-        )
-        factor = jnp.dot(
-            rows, mixing(), precision=HIGHEST, preferred_element_type=jnp.float32
-        )
-        r_ref[...] = factor
-        rms_ref[...] = jnp.sqrt(jnp.sum(factor * factor, axis=0, keepdims=True) / all_cells)
+    def load(n):
+        span = pl.ds(n * group, group)
+        return pltpu.make_async_copy(parts_hbm.at[span], parts.at[span], load_sem.at[n])
+
+    def save(n):
+        span = pl.ds(n * group, group)
+        return pltpu.make_async_copy(q.at[:, span], q_hbm.at[:, span], save_sem.at[n])
+
+    for n in range(blocks // group):
+        load(n).start()
+
+    column = lax.broadcasted_iota(jnp.int32, (height, PAIR * PAIRS), 1)
+    row = lax.broadcasted_iota(jnp.int32, (height, PAIR * PAIRS), 0)
+    spread = jnp.where(
+        row == 16 * (column // PAIR) + lax.rem(column, 16), 1.0, 0.0
+    ).astype(jnp.bfloat16)
+    high, middle = split2(inverse_ref[:, 0:height])
+    order = permutation(height, height).astype(jnp.bfloat16)
+    both = jnp.concatenate(
+        [
+            jnp.dot(order, part, preferred_element_type=jnp.float32).astype(jnp.bfloat16)
+            for part in (high, middle)
+        ],
+        axis=0,
+    )
+    left[...] = jnp.dot(both, spread, preferred_element_type=jnp.float32).astype(jnp.bfloat16)
+    q_rows = q.reshape(COLS * blocks * cells_y, 128)
+
+    def some(n, carry):
+        load(n).wait()
+        for inner in range(group):
+            i = n * group + inner
+            result = jnp.dot(left[...], parts[i], preferred_element_type=jnp.float32)
+            result = result[0:COLS] + result[height : height + COLS]
+            for y in range(cells_y):
+                for c in range(0, COLS, 8):
+                    where = (c * blocks + i) * cells_y + y
+                    q_rows[pl.ds(where, 8, stride=blocks * cells_y), :] = result[
+                        c : c + 8, y * 128 : (y + 1) * 128
+                    ]
+        save(n).start()
+        return carry
+
+    lax.fori_loop(0, blocks // group, some, 0)
+    rows = jnp.dot(
+        permutation(COLS, COLS), factor_ref[:, 0:COLS],
+        precision=HIGHEST, preferred_element_type=jnp.float32,
+    )
+    factor = jnp.dot(rows, mixing(), precision=HIGHEST, preferred_element_type=jnp.float32)
+    r_ref[...] = factor
+    rms_ref[...] = jnp.sqrt(jnp.sum(factor * factor, axis=0, keepdims=True) / all_cells)
+    for n in range(blocks // group):
+        save(n).wait()
 
 
 def orthonormal(all_cells, cells, parts, inverse, factor):
     cells_x, cells_y = cells
-    steps, depth, width = parts.shape
+    blocks, depth, width = parts.shape
+    group = 2
     height = 16 * PAIRS
-    whole = lambda *shape: pl.BlockSpec(shape, lambda i: (0,) * len(shape))
     return pl.pallas_call(
-        functools.partial(orthonormal_kernel, all_cells, cells_y, steps),
-        grid=(steps,),
+        functools.partial(orthonormal_kernel, all_cells, cells_y, blocks, group),
         out_shape=(
-            jax.ShapeDtypeStruct((COLS, steps, cells_y, 128), jnp.float32),
+            jax.ShapeDtypeStruct((COLS, blocks, cells_y, 128), jnp.float32),
             jax.ShapeDtypeStruct((COLS, COLS), jnp.float32),
             jax.ShapeDtypeStruct((1, COLS), jnp.float32),
         ),
         in_specs=[
-            pl.BlockSpec((1, depth, width), lambda i: (i, 0, 0)),
-            whole(height, 128),
-            whole(COLS, 128),
+            pl.BlockSpec(memory_space=pltpu.HBM),
+            pl.BlockSpec(memory_space=VMEM),
+            pl.BlockSpec(memory_space=VMEM),
         ],
         out_specs=(
-            pl.BlockSpec((COLS, 1, cells_y, 128), lambda i: (0, i, 0, 0)),
-            whole(COLS, COLS),
-            whole(1, COLS),
+            pl.BlockSpec(memory_space=pltpu.HBM),
+            pl.BlockSpec(memory_space=VMEM),
+            pl.BlockSpec(memory_space=VMEM),
         ),
         scratch_shapes=[
             VMEM((2 * height, depth), jnp.bfloat16),
+            VMEM(parts.shape, jnp.bfloat16),
+            VMEM((COLS, blocks, cells_y, 128), jnp.float32),
+            pltpu.SemaphoreType.DMA((blocks // group,)),
+            pltpu.SemaphoreType.DMA((blocks // group,)),
         ],
         compiler_params=pltpu.CompilerParams(vmem_limit_bytes=55 * 1024 * 1024),
         name="orthonormal",

time: 85.4 us -> 80.2 us (0.939)
  Pallas kernels: 84.4 us -> 79.4 us
    pallas_call x1, Pallas kernels: 12.8 us -> 7.81 us  [orthonormal(): pl.pallas_call(functools.partial(orthonormal_kernel, all_cells, cells_y,...]
where the time goes in v4:
time: 80.2 us; the launch traced here: 80 us
  Pallas kernels  79.4 us (99%)
    pallas_call x1, Pallas kernels, basis(): pl.pallas_call(functools.partial(basis_kernel, counts, cells), out_shape=...  71.6 us
    pallas_call x1, Pallas kernels, orthonormal(): pl.pallas_call(functools.partial(orthonormal_kernel, all_cells, cells_y,...  7.81 us

profile of v4, /device:TPU:0, one launch (start us, length us, event | category | flops | bytes accessed | tf_op | source)
XLA Modules:
  0.0 80.0 jit_solution(8527798730567623918)
XLA Ops:
  0.6 71.6 %basis.1 = (bf16[16,160,1024]{2,1,0:T(8,128)(2,1)}, f32[80,128]{1,0:T(8,128)}, f32[72,128]{1,0:T(8,128)}) custom-call(s32[256,128]{1,0:T(8,128)} %bitcast.5, f32[1024,128]{1,0:T(8,128)} %bitcast.4, f32[3,4,8,128]{3,2,1,0:T(8,128)} %flow_hbm.1, f32[3,3,4,8,128]{4,3,2,1,0:T(8,128)} %shear_hbm.1), custom_call_target="tpu_custom_call" | custom-call | tf_op jit(solution)/shard_map/basis/pallas_call | solution.py:403
  72.2 7.8 %orthonormal.1 = (f32[72,16,8,128]{3,2,1,0:T(8,128)}, f32[72,72]{1,0:T(8,128)}, f32[1,72]{1,0:T(1,128)}) custom-call(bf16[16,160,1024]{2,1,0:T(8,128)(2,1)} %get-tuple-element.9.parts_hbm, f32[80,128]{1,0:T(8,128)} %get-tuple-element.10.inverse_ref, f32[72,128]{1,0:T(8,128)} %get-tuple-element.11.factor_ref), custom_call_target="tpu_custom_call" | custom-call | tf_op jit(solution)/shard_map/orthonormal/pallas_call | solution.py:517

commit v5 on v4

--- a/solution.py
+++ b/solution.py
@@ -264,8 +264,10 @@
 
             return carry
 
+        lax.fori_loop(1, PIECES - 1, piece_of_faces, 0)
         at_sides(k, 1, "recv")
-        lax.fori_loop(0, PIECES, piece_of_faces, 0)
+        piece_of_faces(0, 0)
+        piece_of_faces(PIECES - 1, 0)
         lax.fori_loop(1, cells_x - 1, y_faces, 0)
 
         if k < S:
@@ -273,7 +275,7 @@
 
         lax.fori_loop(1, cells_y - 1, inside, 0)
 
-    for piece in range(PIECES):
+    for piece in (*range(1, PIECES - 1), 0, PIECES - 1):
         at_sides(1, 0, "start", piece)
     at_sides(1, 1, "start")
     gram[...] = jnp.zeros_like(gram)

time: 80.2 us -> 79.9 us (level)
  no operation moved by 1% of the time
where the time goes in v5:
time: 79.9 us; the launch traced here: 79.7 us
  Pallas kernels  79.1 us (99%)
    pallas_call x1, Pallas kernels, basis(): pl.pallas_call(functools.partial(basis_kernel, counts, cells), out_shape=...  71.3 us
    pallas_call x1, Pallas kernels, orthonormal(): pl.pallas_call(functools.partial(orthonormal_kernel, all_cells, cells_y,...  7.81 us

profile of v5, /device:TPU:0, one launch (start us, length us, event | category | flops | bytes accessed | tf_op | source)
XLA Modules:
  0.0 79.7 jit_solution(16891693973496242037)
XLA Ops:
  0.6 71.3 %basis.1 = (bf16[16,160,1024]{2,1,0:T(8,128)(2,1)}, f32[80,128]{1,0:T(8,128)}, f32[72,128]{1,0:T(8,128)}) custom-call(s32[256,128]{1,0:T(8,128)} %bitcast.5, f32[1024,128]{1,0:T(8,128)} %bitcast.4, f32[3,4,8,128]{3,2,1,0:T(8,128)} %flow_hbm.1, f32[3,3,4,8,128]{4,3,2,1,0:T(8,128)} %shear_hbm.1), custom_call_target="tpu_custom_call" | custom-call | tf_op jit(solution)/shard_map/basis/pallas_call | solution.py:405
  71.9 7.8 %orthonormal.1 = (f32[72,16,8,128]{3,2,1,0:T(8,128)}, f32[72,72]{1,0:T(8,128)}, f32[1,72]{1,0:T(1,128)}) custom-call(bf16[16,160,1024]{2,1,0:T(8,128)(2,1)} %get-tuple-element.9.parts_hbm, f32[80,128]{1,0:T(8,128)} %get-tuple-element.10.inverse_ref, f32[72,128]{1,0:T(8,128)} %get-tuple-element.11.factor_ref), custom_call_target="tpu_custom_call" | custom-call | tf_op jit(solution)/shard_map/orthonormal/pallas_call | solution.py:519
